TPU v7x, 32 devices: a whole 2x2x4 slice. The times are simulated.
32 devices in a mesh: rows: 8 (over y, x, core), grp: 4 (over z).
Axes of the slice: x: 2, y: 2, z: 4, core: 2. Of those that a mesh axis runs over, the one named last changes fastest.
Arguments:
- vector: float32 [128, 16, 384], P(('rows', 'grp')), may hold values from -20 to 20
- near_cols: int32 [128, 3], P(('rows', 'grp')), may hold values from 0 to 127, as said below
- near_blocks: bfloat16 [128, 3, 384, 384], P(('rows', 'grp')), may hold values from -2 to 2
- col_basis: bfloat16 [128, 32, 384], P(('rows', 'grp')), may hold values from -0.3125 to 0.3125
- row_basis: bfloat16 [128, 32, 384], P(('rows', 'grp')), may hold values from -1 to 1
- leaf_far: int32 [128, 8], P(('rows', 'grp')), may hold values from 0 to 127, as said below
- leaf_coupling: bfloat16 [128, 32, 256], P(('rows', 'grp')), may hold values from -0.375 to 0.375
- leaf_transfer: float32 [128, 32, 32], P(('rows', 'grp')), may hold values from -0.5 to 0.5
- box_far: int32 [32, 4], P(('rows', 'grp')), may hold values from 0 to 31, as said below
- box_coupling: bfloat16 [32, 32, 128], P(('rows', 'grp')), may hold values from -0.5 to 0.5
- box_transfer: float32 [32, 32, 32], P(('rows', 'grp')), may hold values from -1 to 1
- coarse_far: int32 [8, 4], P('rows'), may hold values from 0 to 7, as said below
- coarse_coupling: bfloat16 [8, 32, 128], P('rows'), may hold values from -0.5 to 0.5
Outputs:
- basis: float32 [128, 16, 384], P(('rows', 'grp'))
- remainder: float32 [128, 16, 384], P(('rows', 'grp'))
- hessenberg: float32 [16, 5], replicated
Inputs may be any that keep to these rules, and one draw needn't show every extreme that they name: `near_cols`: entry 0 of leaf l is l itself; the other entries are distinct leaves l + o with 0 < |o| <= 4. `leaf_far`: the entries of leaf l are distinct leaves g with |g - l| > 4 and |g // 16 - l // 16| <= 1. `box_far`: the entries of box x are distinct boxes y with |y - x| > 1 and |y // 4 - x // 4| <= 1. `coarse_far`: the entries of group g are distinct groups h with |h - g| > 1.
All inputs are finite; a program needn't handle non-finite values.
Results may differ from a plain program's by a relative error of at most 0.015.
Values may be sent and summed in bfloat16 or wider, within the bound.
A program may use at most 64 MiB of HBM per device.

v0:
```python
import jax
import jax.numpy as jnp
from jax import lax
from jax.sharding import PartitionSpec as P

R = 32


highest = lax.Precision.HIGHEST
epsilon = 1e-06


def padded(block, sides, width):
    for axis, dim in sides:
        count = lax.axis_size(axis)
        forward = [(i, i + 1) for i in range(count - 1)]
        backward = [(target, source) for source, target in forward]
        low = lax.ppermute(
            lax.slice_in_dim(block, block.shape[dim] - width, None, axis=dim), axis, forward
        )
        high = lax.ppermute(lax.slice_in_dim(block, 0, width, axis=dim), axis, backward)
        block = jnp.concatenate([low, block, high], axis=dim)
    return block


def pick_flat(source, indices):
    chosen = jnp.take(source, indices, axis=0)
    target_count, slot_count = indices.shape
    chosen = chosen.reshape(target_count, slot_count, -1, R)
    chosen = jnp.transpose(chosen, (0, 2, 1, 3))
    return chosen.reshape(target_count, -1, slot_count * R)


def shards(
    vector,
    near_cols,
    near_blocks,
    col_basis,
    row_basis,
    leaf_far,
    leaf_coupling,
    leaf_transfer,
    box_far,
    box_coupling,
    box_transfer,
    coarse_far,
    coarse_coupling,
):
    leaf_count, rhs_count, cell_count = vector.shape
    group_size = lax.axis_size("grp")
    row_count = lax.axis_size("rows")
    row_index = lax.axis_index("rows")
    device = row_index * group_size + lax.axis_index("grp")
    first_leaf = device * leaf_count
    total_count = leaf_count * row_count * group_size * cell_count
    coef_width = rhs_count * R

    def apply_operator(field):
        field_bf = field.astype(jnp.bfloat16)
        widened = padded(field_bf, ((("rows", "grp"), 0),), leaf_count)
        picked = jnp.take(widened, near_cols - (first_leaf - leaf_count), axis=0)
        near_sum = jnp.einsum(
            "lkbj,lkij->lbi", picked, near_blocks, preferred_element_type=jnp.float32
        )
        leaf_coef = jnp.einsum(
            "lbj,lrj->lbr", field_bf, col_basis, preferred_element_type=jnp.float32
        ).astype(jnp.bfloat16)
        box_coef = jnp.einsum(
            "lbr,lrs->bs", leaf_coef.astype(jnp.float32), leaf_transfer, precision=highest
        ).astype(jnp.bfloat16)
        parent_part = jnp.dot(
            box_coef.astype(jnp.float32), box_transfer[0], precision=highest
        ).astype(jnp.bfloat16)
        leaf_rows = leaf_coef.reshape(leaf_count, coef_width)
        box_row = box_coef.reshape(1, coef_width)
        parent_row = parent_part.reshape(1, coef_width)
        packed = jnp.concatenate([leaf_rows, box_row, parent_row], axis=0)
        gathered = lax.all_gather(packed, ("rows", "grp"), axis=0, tiled=True)
        gathered = gathered.reshape(row_count * group_size, leaf_count + 2, coef_width)
        leaf_source = gathered[:, :leaf_count].reshape(-1, coef_width)
        box_source = gathered[:, leaf_count]
        group_all = (
            gathered[:, leaf_count + 1]
            .astype(jnp.float32)
            .reshape(row_count, group_size, coef_width)
        )
        group_all = group_all.sum(axis=1).astype(jnp.bfloat16)
        leaf_field = jnp.einsum(
            "lbm,lrm->lbr",
            pick_flat(leaf_source, leaf_far),
            leaf_coupling,
            preferred_element_type=jnp.float32,
        )
        box_field = jnp.einsum(
            "xbm,xrm->xbr",
            pick_flat(box_source, box_far),
            box_coupling,
            preferred_element_type=jnp.float32,
        )[0]
        group_field = jnp.einsum(
            "gbm,grm->gbr",
            pick_flat(group_all, coarse_far),
            coarse_coupling,
            preferred_element_type=jnp.float32,
        )[0]
        box_local = box_field + jnp.einsum(
            "bs,rs->br", group_field, box_transfer[0], precision=highest
        )
        leaf_local = leaf_field + jnp.einsum(
            "bs,lrs->lbr", box_local, leaf_transfer, precision=highest
        )
        leaf_local = leaf_local.astype(jnp.bfloat16)
        far_sum = jnp.einsum(
            "lbr,lrj->lbj", leaf_local, row_basis, preferred_element_type=jnp.float32
        )
        return 0.5 * field + near_sum + far_sum

    def stacked_means(pairs):
        partial_sums = jnp.stack(
            [jnp.sum(left * right, axis=(0, 2)) for left, right in pairs], axis=0
        )
        return lax.psum(partial_sums, ("rows", "grp")) / total_count

    def spread_rhs(values):
        return values[None, :, None]

    norm_first = jnp.sqrt(stacked_means([(vector, vector)])[0] + epsilon)
    first_basis = vector / spread_rhs(norm_first)
    image_one = apply_operator(first_basis)
    first_gram = stacked_means(
        [(first_basis, image_one), (image_one, image_one), (first_basis, first_basis)]
    )
    proj_first = first_gram[0]
    first_square = first_gram[2]
    image_one = image_one - spread_rhs(proj_first) * first_basis
    image_square = first_gram[1] - proj_first * proj_first * (2.0 - first_square)
    norm_image = jnp.sqrt(image_square + epsilon)
    basis = image_one / spread_rhs(norm_image)
    remainder = apply_operator(basis)
    second_gram = stacked_means(
        [
            (first_basis, remainder),
            (basis, remainder),
            (remainder, remainder),
            (basis, first_basis),
            (basis, basis),
        ]
    )
    first_with = second_gram[0]
    basis_with = second_gram[1]
    image_square_two = second_gram[2]
    cross_term = second_gram[3]
    basis_square = second_gram[4]
    proj_basis = basis_with - first_with * cross_term
    remainder = remainder - spread_rhs(first_with) * first_basis
    remainder = remainder - spread_rhs(proj_basis) * basis
    last_square = (
        image_square_two
        + first_with * first_with * first_square
        + proj_basis * proj_basis * basis_square
        - 2.0 * first_with * first_with
        - 2.0 * proj_basis * basis_with
        + 2.0 * first_with * proj_basis * cross_term
    )
    norm_last = jnp.sqrt(last_square + epsilon)
    hessenberg = jnp.stack([proj_first, norm_image, first_with, proj_basis, norm_last], axis=1)
    return (basis, remainder, hessenberg)


def solution(mesh):
    return jax.shard_map(
        shards,
        mesh=mesh,
        in_specs=(
            P(("rows", "grp"), None, None),
            P(("rows", "grp"), None),
            P(("rows", "grp"), None, None, None),
            P(("rows", "grp"), None, None),
            P(("rows", "grp"), None, None),
            P(("rows", "grp"), None),
            P(("rows", "grp"), None, None),
            P(("rows", "grp"), None, None),
            P(("rows", "grp"), None),
            P(("rows", "grp"), None, None),
            P(("rows", "grp"), None, None),
            P("rows", None),
            P("rows", None, None),
        ),
        out_specs=(P(("rows", "grp"), None, None), P(("rows", "grp"), None, None), P()),
        check_vma=False,
    )
```

profile of v0, /device:TPU:0, one launch (start us, length us, event | category | flops | bytes accessed | tf_op | source)
XLA Modules:
  0.0 395.3 jit_solution(10458650043216176605)
XLA Ops:
  1.8 42.0 %psum.21 = f32[1,16]{1,0:T(1,128)S(1)} all-reduce(f32[1,16]{1,0:T(1,128)S(1)} %bitcast.244), channel_id=1, replica_groups=mesh['rows'=8,'grp'=4] {'rows','grp'}, use_global_device_ids=true, to_apply=%region_1.0 | all-reduce | flops 16 | bytes 128 | tf_op jit(solution)/shard_map/psum | solution.py:122
  43.8 1.6 fusion.44
  45.4 4.0 %collective-permute-start = (bf16[4,16,384]{2,1,0:T(8,128)(2,1)}, bf16[4,16,384]{2,1,0:T(8,128)(2,1)}, u32[]{:S(2)}, u32[]{:S(2)}) collective-permute-start(bf16[4,16,384]{2,1,0:T(8,128)(2,1)} %fusion.44), channel_id=1, source_target_pairs={{0,1},{1,2},{2,3},{3,4},{4,5},{5,6},{6,7},{7,8},{8,9},{9,10},{10,1... | collective-permute-start | bytes 147464 | tf_op jit(solution)/shard_map/ppermute | solution.py:18
  49.5 1.3 collective-permute-start.1
  57.4 1.6 fusion.8
  61.5 68.6 %all-gather = bf16[32,6,512]{2,1,0:T(8,128)(2,1)S(1)} all-gather(bf16[1,6,512]{2,1,0:T(8,128)(2,1)S(1)} %maximum_bitcast_fusion), channel_id=1, replica_groups=mesh['rows'=8,'grp'=4] {'rows','grp'}, dimensions={0}, use_global_device_ids=true | all-gather | bytes 202752 | tf_op jit(solution)/shard_map/all_gather | solution.py:78
  130.0 1.4 slice_reduce_fusion.1
  134.6 1.4 squeeze.51
  137.9 1.3 bitcast_select_fusion.4
  140.7 1.4 reshape.428
  142.0 1.4 copy.65
  144.2 1.3 gather_fusion.2
  145.5 1.3 bitcast_select_fusion.5
  148.2 1.4 reshape.425
  149.6 1.6 reshape.421
  151.2 1.3 reshape.527
  153.7 2.3 gather_fusion.1
  156.0 1.4 bitcast_select_fusion.1
  157.4 1.5 reshape.422
  159.0 1.6 copy.44
  160.6 1.7 reshape.423
  162.2 1.3 compare_and_fusion.1
  163.5 1.3 reshape.523
  168.4 1.8 fusion.4
  170.2 1.3 pad_clamp_fusion.3
  171.5 1.5 pad_maximum_fusion
  173.0 2.3 gather_fusion
  175.2 2.1 fusion.1
  178.9 41.2 %psum.22 = f32[3,16]{1,0:T(4,128)} all-reduce(f32[3,16]{1,0:T(4,128)} %pad_maximum_fusion.2), channel_id=1, replica_groups=mesh['rows'=8,'grp'=4] {'rows','grp'}, use_global_device_ids=true, to_apply=%region_6.11 | all-reduce | flops 48 | bytes 384 | tf_op jit(solution)/shard_map/psum | solution.py:122
  221.4 1.7 fusion.46
  227.8 1.4 reshape.431
  229.1 1.4 reshape.430
  230.5 1.3 reshape.432
  232.6 67.5 %all-gather.1 = bf16[32,6,512]{2,1,0:T(8,128)(2,1)S(1)} all-gather(bf16[1,6,512]{2,1,0:T(8,128)(2,1)S(1)} %maximum_bitcast_fusion.1), channel_id=1, replica_groups=mesh['rows'=8,'grp'=4] {'rows','grp'}, dimensions={0}, use_global_device_ids=true | all-gather | bytes 202752 | tf_op jit(solution)/shard_map/all_gather | solution.py:78
  300.1 1.4 slice_reduce_fusion
  302.1 2.7 collective-permute-start.2
  304.8 1.3 collective-permute-start.3
  306.1 1.4 squeeze.54
  307.5 1.4 reduce_sum.110
  308.9 2.0 gather_fusion.7
  310.9 1.4 bitcast_select_fusion.2
  312.2 1.4 reshape.439
  313.6 1.3 copy.66
  314.9 1.4 reshape.440
  316.3 1.4 fusion.20
  317.7 1.4 copy.64
  319.2 2.0 gather_fusion.6
  321.2 1.4 bitcast_select_fusion.3
  322.6 1.4 reshape.437
  323.9 1.3 copy.67
  325.3 1.4 reshape.438
  326.7 1.4 fusion.24
  328.1 1.6 reshape.434
  329.7 2.3 gather_fusion.5
  332.0 1.4 bitcast_select_fusion
  333.4 1.5 reshape.435
  334.9 1.6 copy.48
  336.5 1.7 reshape.436
  341.3 1.5 pad_maximum_fusion.1
  342.8 2.3 gather_fusion.4
  345.1 2.1 fusion
  347.2 1.6 multiply_reduce_fusion.1
  349.5 42.1 %psum.23 = f32[5,16]{1,0:T(8,128)S(1)} all-reduce(f32[5,16]{1,0:T(8,128)S(1)} %stack.49), channel_id=1, replica_groups=mesh['rows'=8,'grp'=4] {'rows','grp'}, use_global_device_ids=true, to_apply=%region_13.18 | all-reduce | flops 80 | bytes 640 | tf_op jit(solution)/shard_map/psum | solution.py:122
  392.4 1.7 multiply_subtract_fusion
  (85 shorter events, 38.3 us)
Async XLA Ops:
  0.6 174.6 %copy-start = (bf16[4,3,384,384]{3,2,1,0:T(8,128)(2,1)S(1)}, bf16[4,3,384,384]{3,2,1,0:T(8,128)(2,1)}, u32[]{:S(2)}) copy-start(bf16[4,3,384,384]{3,2,1,0:T(8,128)(2,1)} %param.23) | copy-start | bytes 10616836
  43.8 10.6 %copy-start.10 = (f32[16]{0:T(128)}, f32[16]{0:T(128)S(1)}, u32[]{:S(2)}) copy-start(f32[16]{0:T(128)S(1)} %sqrt_bitcast_fusion) | copy-start | bytes 196
  45.4 126.0 %collective-permute-start = (bf16[4,16,384]{2,1,0:T(8,128)(2,1)}, bf16[4,16,384]{2,1,0:T(8,128)(2,1)}, u32[]{:S(2)}, u32[]{:S(2)}) collective-permute-start(bf16[4,16,384]{2,1,0:T(8,128)(2,1)} %fusion.44), channel_id=1, source_target_pairs={{0,1},{1,2},{2,3},{3,4},{4,5},{5,6},{6,7},{7,8},{8,9},{9,10},{10,1... | collective-permute-start | bytes 147464 | tf_op jit(solution)/shard_map/ppermute | solution.py:18
  49.5 122.0 %collective-permute-start.1 = (bf16[4,16,384]{2,1,0:T(8,128)(2,1)}, bf16[4,16,384]{2,1,0:T(8,128)(2,1)}, u32[]{:S(2)}, u32[]{:S(2)}) collective-permute-start(bf16[4,16,384]{2,1,0:T(8,128)(2,1)} %fusion.44), channel_id=1, source_target_pairs={{1,0},{2,1},{3,2},{4,3},{5,4},{6,5},{7,6},{8,7},{9,8},{10,9},{11,1... | collective-permute-start | bytes 147464 | tf_op jit(solution)/shard_map/ppermute | solution.py:21
  136.5 1.4 copy-start.13
  144.2 1.3 copy-start.14
  151.2 75.8 %copy-start.5 = (f32[1,32,32]{2,1,0:T(8,128)S(1)}, f32[1,32,32]{2,1,0:T(8,128)}, u32[]{:S(2)}) copy-start(f32[1,32,32]{2,1,0:T(8,128)} %param.31) | copy-start | bytes 12292
  175.2 2.1 copy-start.1
  175.2 2.1 copy-start.8
  175.2 2.2 copy-start.11
  175.2 2.2 copy-start.15
  220.9 0.6 copy-start.9
  223.1 0.6 copy-start.4
  224.8 0.6 copy-start.6
  226.4 0.6 copy-start.7
  302.1 39.1 %collective-permute-start.2 = (bf16[4,16,384]{2,1,0:T(8,128)(2,1)}, bf16[4,16,384]{2,1,0:T(8,128)(2,1)}, u32[]{:S(2)}, u32[]{:S(2)}) collective-permute-start(bf16[4,16,384]{2,1,0:T(8,128)(2,1)} %copy-done.4), channel_id=1, source_target_pairs={{0,1},{1,2},{2,3},{3,4},{4,5},{5,6},{6,7},{7,8},{8,9},{9,10},{10,1... | collective-permute-start | bytes 147464 | tf_op jit(solution)/shard_map/ppermute | solution.py:18
  304.8 36.5 %collective-permute-start.3 = (bf16[4,16,384]{2,1,0:T(8,128)(2,1)}, bf16[4,16,384]{2,1,0:T(8,128)(2,1)}, u32[]{:S(2)}, u32[]{:S(2)}) collective-permute-start(bf16[4,16,384]{2,1,0:T(8,128)(2,1)} %copy-done.4), channel_id=1, source_target_pairs={{1,0},{2,1},{3,2},{4,3},{5,4},{6,5},{7,6},{8,7},{9,8},{10,9},{11,1... | collective-permute-start | bytes 147464 | tf_op jit(solution)/shard_map/ppermute | solution.py:21
  345.1 2.1 copy-start.2
  345.1 2.1 copy-start.3
  345.1 2.1 copy-start.12
  345.1 2.1 copy-start.16
where the time goes:
time: 400 us; the launch traced here: 395 us
  blocking collectives  261 us (65%)
  local copies, waits for them, and re-layouts  63.9 us (16%)
  other arithmetic  35.6 us (9%)
  matrix products  24.3 us (6%)
  starting transfers between devices  9.28 us (2%)
    all_gather x2, blocking collectives, apply_operator(): gathered = lax.all_gather(packed, ('rows', 'grp'), axis=0, tiled=True)  136 us
    psum x3, blocking collectives, stacked_means(): return lax.psum(partial_sums, ('rows', 'grp')) / total_count  125 us
    reshape x10, local copies, waits for them, and re-layouts, pick_flat(): chosen = chosen.reshape(target_count, slot_count, -1, R)  11.2 us
    gather x6, local copies, waits for them, and re-layouts, pick_flat(): chosen = jnp.take(source, indices, axis=0)  10.5 us
    select_n x7, other arithmetic, pick_flat(): chosen = jnp.take(source, indices, axis=0)  9.48 us
  transfers between devices with their start and end apart: 4, of which 0 were waited for; matrix products, arithmetic and copies ran while one was open for 22% of the time, Pallas kernels for 0%

commit v1 on v0

v1 whole, which is shorter than its diff:
```python
import functools

import jax
import jax.numpy as jnp
from jax import lax
from jax.experimental import pallas as pl
from jax.experimental.pallas import tpu as pltpu
from jax.sharding import PartitionSpec as P

LANES = 128
epsilon = 1e-06
highest = lax.Precision.HIGHEST
MESH = pl.DeviceIdType.MESH
bf16 = jnp.bfloat16
f32 = jnp.float32


def nt(left, right, precision=None):
    return lax.dot_general(
        left, right, (((1,), (1,)), ((), ())), precision=precision, preferred_element_type=f32
    )


def spread_matrix(rows, slots, rank, low, copies):
    shape = (rows, slots * LANES)
    row = lax.broadcasted_iota(jnp.int32, shape, 0)
    column = lax.broadcasted_iota(jnp.int32, shape, 1)
    lane = column % LANES - low
    wanted = (column // LANES) * rank + lane % rank
    hit = (row == wanted) & (lane >= 0) & (lane < copies * rank)
    return jnp.where(hit, 1.0, 0.0).astype(bf16)


def kernel(
    rows,
    grp,
    *refs,
):
    sources = refs[:13]
    basis_out, remainder_out, hessenberg_out = refs[13:16]
    targets = refs[16:29]
    (
        near_cols,
        leaf_far,
        box_far,
        coarse_far,
        vector,
        near_blocks,
        col_basis,
        row_basis,
        leaf_coupling,
        leaf_transfer,
        box_coupling,
        box_transfer,
        coarse_coupling,
    ) = targets
    (
        field_a,
        field_b,
        coef_a,
        coef_b,
        group_a,
        group_b,
        sums_a,
        sums_b,
        send_basis,
        receive_basis,
        leaf_weights,
        box_weights,
        group_weights,
        image,
        image_two,
        load_sem,
        field_send,
        field_recv,
        coef_send,
        coef_recv,
        group_send,
        group_recv,
        sums_send,
        sums_recv,
    ) = refs[29:]
    leaves, rhs, cells = vector.shape
    rank = col_basis.shape[1]
    near_count = near_cols.shape[1]
    leaf_slots = leaf_far.shape[1]
    box_slots = box_far.shape[1]
    coarse_slots = coarse_far.shape[1]
    devices = rows * grp
    total_count = leaves * devices * cells
    row = lax.axis_index("rows")
    z = lax.axis_index("grp")
    me = row * grp + z

    loads = [
        pltpu.make_async_copy(source, target, load_sem.at[n])
        for n, (source, target) in enumerate(zip(sources, targets))
    ]
    for n in (4, 6, 9, 11, 7, 8, 10, 12, 0, 1, 2, 3, 5):
        loads[n].start()

    barrier = pltpu.get_barrier_semaphore()

    def greet(step, carry):
        other = lax.rem(me + step, devices)
        pl.semaphore_signal(
            barrier,
            inc=1,
            device_id=(lax.div(other, grp), lax.rem(other, grp)),
            device_id_type=MESH,
        )
        return carry

    lax.fori_loop(1, devices, greet, 0)

    send_basis[...] = jnp.zeros_like(send_basis)
    for n in (4, 6, 9, 11):
        loads[n].wait()
    for l in range(leaves):
        send_basis[l * rank : (l + 1) * rank, l * cells : (l + 1) * cells] = col_basis[l]
    width = leaves * rank
    transfer = leaf_transfer[...].reshape(width, rank)
    up_box = lax.dot_general(
        transfer,
        send_basis[:width].astype(f32),
        (((0,), (0,)), ((), ())),
        precision=highest,
        preferred_element_type=f32,
    )
    up_parent = lax.dot_general(
        box_transfer[0],
        up_box,
        (((0,), (0,)), ((), ())),
        precision=highest,
        preferred_element_type=f32,
    )
    send_basis[width : width + rank] = up_box.astype(bf16)
    send_basis[width + rank : width + 2 * rank] = up_parent.astype(bf16)

    def prepare_receive():
        for n in (7, 8, 10, 12, 0, 1, 2, 3):
            loads[n].wait()
        receive_basis[...] = jnp.zeros_like(receive_basis)
        for l in range(leaves):
            receive_basis[l * rank : (l + 1) * rank, l * cells : (l + 1) * cells] = row_basis[l]
        tiled = jnp.dot(
            leaf_coupling[...].reshape(width, leaf_slots * rank),
            spread_matrix(leaf_slots * rank, leaf_slots, rank, 0, leaves),
            preferred_element_type=f32,
        )
        part = lax.broadcasted_iota(jnp.int32, (rank, LANES), 1) // rank
        for l in range(leaves):
            for k in range(leaf_slots):
                sub = lax.rem(leaf_far[l, k], leaves)
                piece = tiled[l * rank : (l + 1) * rank, k * LANES : (k + 1) * LANES]
                leaf_weights[l, :, k * LANES : (k + 1) * LANES] = jnp.where(
                    part == sub, piece, 0.0
                ).astype(bf16)
        box_wide = jnp.dot(
            box_coupling[0],
            spread_matrix(box_slots * rank, box_slots, rank, 0, 1),
            preferred_element_type=f32,
        )
        box_weights[...] = jnp.dot(
            transfer, box_wide, precision=highest, preferred_element_type=f32
        ).astype(bf16)
        group_wide = jnp.dot(
            coarse_coupling[0],
            spread_matrix(coarse_slots * rank, coarse_slots, rank, rank, 1),
            preferred_element_type=f32,
        )
        down = jnp.dot(transfer, box_transfer[0], precision=highest, preferred_element_type=f32)
        group_weights[...] = jnp.dot(
            down, group_wide, precision=highest, preferred_element_type=f32
        ).astype(bf16)

    def send(src, dst, send_sem, recv_sem, to_row, to_z):
        pltpu.make_async_remote_copy(
            src_ref=src,
            dst_ref=dst,
            send_sem=send_sem,
            recv_sem=recv_sem,
            device_id=(to_row, to_z),
            device_id_type=MESH,
        ).start()

    def wait_bytes(ref, sem):
        pltpu.make_async_copy(ref, ref, sem).wait()

    def operator(phase, source, result, field, coef, group, after_send, before_near):
        for l in range(leaves):
            field[leaves + l] = source[l].astype(bf16)
        if phase == 0:
            pl.semaphore_wait(barrier, devices - 1)
        own = field.at[pl.ds(leaves, leaves)]
        low = field.at[pl.ds(0, leaves)]
        high = field.at[pl.ds(2 * leaves, leaves)]

        @pl.when(me < devices - 1)
        def _():
            other = me + 1
            send(
                own,
                low,
                field_send.at[phase, 0],
                field_recv.at[phase, 0],
                lax.div(other, grp),
                lax.rem(other, grp),
            )

        @pl.when(me > 0)
        def _():
            other = me - 1
            send(
                own,
                high,
                field_send.at[phase, 1],
                field_recv.at[phase, 1],
                lax.div(other, grp),
                lax.rem(other, grp),
            )

        wide = jnp.concatenate([field[leaves + l] for l in range(leaves)], axis=1)
        sent = nt(wide, send_basis[...]).astype(bf16)
        mine = grp + z
        coef[mine, 0] = sent[:, :LANES]
        coef[mine, 1] = sent[:, LANES:]

        for step in range(1, grp):
            send(
                coef.at[mine],
                coef.at[mine],
                coef_send.at[phase, 1],
                coef_recv.at[phase, 1],
                row,
                lax.rem(z + step, grp),
            )

        @pl.when(row > 0)
        def _():
            for other in range(grp):
                send(
                    coef.at[mine],
                    coef.at[2 * grp + z],
                    coef_send.at[phase, 0],
                    coef_recv.at[phase, 2],
                    row - 1,
                    other,
                )

        @pl.when(row < rows - 1)
        def _():
            for other in range(grp):
                send(
                    coef.at[mine],
                    coef.at[z],
                    coef_send.at[phase, 2],
                    coef_recv.at[phase, 0],
                    row + 1,
                    other,
                )

        after_send()
        before_near()
        for l in range(leaves):
            result[l] = nt(field[leaves + l], near_blocks[l, 0])

        if grp > 1:
            wait_bytes(coef.at[pl.ds(0, grp - 1)], coef_recv.at[phase, 1])
        together = coef[grp, 1].astype(f32)
        for other in range(1, grp):
            together = together + coef[grp + other, 1].astype(f32)
        group[row] = together.astype(bf16)

        def send_group(step, carry):
            send(
                group.at[row],
                group.at[row],
                group_send.at[phase],
                group_recv.at[phase],
                lax.rem(row + step, rows),
                z,
            )
            return carry

        lax.fori_loop(1, rows, send_group, 0)

        @pl.when(me > 0)
        def _():
            wait_bytes(low, field_recv.at[phase, 0])

        @pl.when(me < devices - 1)
        def _():
            wait_bytes(high, field_recv.at[phase, 1])

        first = me * leaves - leaves
        for l in range(leaves):
            total = result[l]
            for k in range(1, near_count):
                total = total + nt(field[jnp.clip(near_cols[l, k] - first, 0, 3 * leaves - 1)], near_blocks[l, k])
            result[l] = total

        @pl.when(row > 0)
        def _():
            wait_bytes(coef.at[pl.ds(0, grp)], coef_recv.at[phase, 0])

        @pl.when(row < rows - 1)
        def _():
            wait_bytes(coef.at[pl.ds(0, grp)], coef_recv.at[phase, 2])

        def slot(box):
            return jnp.clip(box - (row * grp - grp), 0, 3 * grp - 1)

        parts = []
        for l in range(leaves):
            picked = jnp.concatenate(
                [
                    coef[slot(lax.div(leaf_far[l, k], leaves)), 0]
                    for k in range(leaf_slots)
                ],
                axis=1,
            )
            parts.append(nt(picked, leaf_weights[l]))
        local = jnp.concatenate(parts, axis=1)
        picked = jnp.concatenate(
            [coef[slot(box_far[0, k]), 1] for k in range(box_slots)], axis=1
        )
        local = local + nt(picked, box_weights[...])
        if rows > 1:
            wait_bytes(group.at[pl.ds(0, rows - 1)], group_recv.at[phase])
        picked = jnp.concatenate([group[coarse_far[0, k]] for k in range(coarse_slots)], axis=1)
        local = local + nt(picked, group_weights[...])
        far = jnp.dot(local.astype(bf16), receive_basis[...], preferred_element_type=f32)
        for l in range(leaves):
            result[l] = result[l] + far[:, l * cells : (l + 1) * cells]

    def drain(phase, field, coef, group):
        own = field.at[pl.ds(leaves, leaves)]

        @pl.when(me < devices - 1)
        def _():
            wait_bytes(own, field_send.at[phase, 0])

        @pl.when(me > 0)
        def _():
            wait_bytes(own, field_send.at[phase, 1])

        @pl.when(row > 0)
        def _():
            wait_bytes(coef.at[pl.ds(0, grp)], coef_send.at[phase, 0])

        if grp > 1:
            wait_bytes(coef.at[pl.ds(0, grp - 1)], coef_send.at[phase, 1])

        @pl.when(row < rows - 1)
        def _():
            wait_bytes(coef.at[pl.ds(0, grp)], coef_send.at[phase, 2])

        if rows > 1:
            wait_bytes(group.at[pl.ds(0, rows - 1)], group_send.at[phase])

    sub_at = lax.broadcasted_iota(jnp.int32, (rhs, LANES), 0)
    lane_at = lax.broadcasted_iota(jnp.int32, (rhs, LANES), 1)

    def start_sums(index, sums, products):
        spread = jnp.zeros((rhs, LANES), f32)
        for n, product in enumerate(products):
            column = jnp.sum(product, axis=1, keepdims=True)
            spread = jnp.where(lane_at == sub_at + n * rhs, column, spread)
        sums[me] = jnp.sum(spread, axis=0, keepdims=True)

        def send_sums(step, carry):
            other = lax.rem(me + step, devices)
            send(
                sums.at[me],
                sums.at[me],
                sums_send.at[index],
                sums_recv.at[index],
                lax.div(other, grp),
                lax.rem(other, grp),
            )
            return carry

        lax.fori_loop(1, devices, send_sums, 0)

    def finish_sums(index, sums, count):
        wait_bytes(sums.at[pl.ds(0, devices - 1)], sums_recv.at[index])
        line = jnp.sum(sums[...], axis=0) / total_count
        spread = jnp.broadcast_to(line, (rhs, LANES))
        return [
            jnp.sum(jnp.where(lane_at == sub_at + n * rhs, spread, 0.0), axis=1, keepdims=True)
            for n in range(count)
        ]

    def products(pairs):
        sums = []
        for left, right in pairs:
            total = left[0] * right[0]
            for l in range(1, leaves):
                total = total + left[l] * right[l]
            sums.append(total)
        return sums

    def start_first_sums():
        start_sums(
            0, sums_a, products([(vector, vector), (vector, image), (image, image)])
        )

    operator(0, vector, image, field_a, coef_a, group_a, prepare_receive, loads[5].wait)
    operator(
        1, image, image_two, field_b, coef_b, group_b, start_first_sums, lambda: None
    )

    vv, vu, uu = finish_sums(0, sums_a, 3)
    norm_first = jnp.sqrt(vv + epsilon)
    scale_first = 1.0 / norm_first
    first_square = vv * scale_first * scale_first
    proj_first = (0.5 * vv + vu) * scale_first * scale_first
    shift = 0.5 - proj_first
    image_square = (uu + 2.0 * shift * vu + shift * shift * vv) * scale_first * scale_first
    norm_image = jnp.sqrt(jnp.maximum(image_square, 0.0) + epsilon)
    scale = scale_first / norm_image
    for l in range(leaves):
        basis = (image[l] + shift * vector[l]) * scale
        basis_out[l] = basis
        remainder_out[l] = 0.5 * basis + (image_two[l] + shift * image[l]) * scale
    start_sums(
        1,
        sums_b,
        products(
            [
                (vector, remainder_out),
                (basis_out, remainder_out),
                (remainder_out, remainder_out),
                (basis_out, vector),
                (basis_out, basis_out),
            ]
        ),
    )
    drain(0, field_a, coef_a, group_a)
    drain(1, field_b, coef_b, group_b)
    wait_bytes(sums_a.at[pl.ds(0, devices - 1)], sums_send.at[0])
    first_with, basis_with, square_two, cross_term, basis_square = finish_sums(1, sums_b, 5)
    first_with = first_with * scale_first
    cross_term = cross_term * scale_first
    proj_basis = basis_with - first_with * cross_term
    first_part = first_with * scale_first
    for l in range(leaves):
        remainder_out[l] = (
            remainder_out[l] - first_part * vector[l] - proj_basis * basis_out[l]
        )
    last_square = (
        square_two
        + first_with * first_with * first_square
        + proj_basis * proj_basis * basis_square
        - 2.0 * first_with * first_with
        - 2.0 * proj_basis * basis_with
        + 2.0 * first_with * proj_basis * cross_term
    )
    norm_last = jnp.sqrt(jnp.maximum(last_square, 0.0) + epsilon)
    for n, entry in enumerate([proj_first, norm_image, first_with, proj_basis, norm_last]):
        line = jnp.sum(jnp.where(lane_at == sub_at, entry, 0.0), axis=0, keepdims=True)
        hessenberg_out[n : n + 1, :] = line[:, :rhs]
    wait_bytes(sums_b.at[pl.ds(0, devices - 1)], sums_send.at[1])


def shards(
    rows,
    grp,
    vector,
    near_cols,
    near_blocks,
    col_basis,
    row_basis,
    leaf_far,
    leaf_coupling,
    leaf_transfer,
    box_far,
    box_coupling,
    box_transfer,
    coarse_far,
    coarse_coupling,
):
    leaves, rhs, cells = vector.shape
    rank = col_basis.shape[1]
    devices = rows * grp
    assert leaves * rank == LANES and box_far.shape[0] == 1 and coarse_far.shape[0] == 1
    assert 5 * rhs <= LANES
    vmem = pl.BlockSpec(memory_space=pltpu.VMEM)
    dma = pltpu.SemaphoreType.DMA
    operands = (
        near_cols,
        leaf_far,
        box_far,
        coarse_far,
        vector,
        near_blocks,
        col_basis,
        row_basis,
        leaf_coupling,
        leaf_transfer,
        box_coupling,
        box_transfer,
        coarse_coupling,
    )
    basis, remainder, entries = pl.pallas_call(
        functools.partial(kernel, rows, grp),
        out_shape=(
            jax.ShapeDtypeStruct(vector.shape, f32),
            jax.ShapeDtypeStruct(vector.shape, f32),
            jax.ShapeDtypeStruct((5, rhs), f32),
        ),
        in_specs=[pl.BlockSpec(memory_space=pltpu.HBM)] * len(operands),
        out_specs=(vmem, vmem, vmem),
        scratch_shapes=[
            *[pltpu.SMEM(operand.shape, operand.dtype) for operand in operands[:4]],
            *[pltpu.VMEM(operand.shape, operand.dtype) for operand in operands[4:]],
            pltpu.VMEM((3 * leaves, rhs, cells), bf16),
            pltpu.VMEM((3 * leaves, rhs, cells), bf16),
            pltpu.VMEM((3 * grp, 2, rhs, LANES), bf16),
            pltpu.VMEM((3 * grp, 2, rhs, LANES), bf16),
            pltpu.VMEM((rows, rhs, LANES), bf16),
            pltpu.VMEM((rows, rhs, LANES), bf16),
            pltpu.VMEM((devices, 1, LANES), f32),
            pltpu.VMEM((devices, 1, LANES), f32),
            pltpu.VMEM((2 * LANES, leaves * cells), bf16),
            pltpu.VMEM((LANES, leaves * cells), bf16),
            pltpu.VMEM((leaves, rank, leaf_far.shape[1] * LANES), bf16),
            pltpu.VMEM((LANES, box_far.shape[1] * LANES), bf16),
            pltpu.VMEM((LANES, coarse_far.shape[1] * LANES), bf16),
            pltpu.VMEM(vector.shape, f32),
            pltpu.VMEM(vector.shape, f32),
            dma((len(operands),)),
            dma((2, 2)),
            dma((2, 2)),
            dma((2, 3)),
            dma((2, 3)),
            dma((2,)),
            dma((2,)),
            dma((2,)),
            dma((2,)),
        ],
        compiler_params=pltpu.CompilerParams(
            collective_id=0, has_side_effects=True, vmem_limit_bytes=65100 * 1024
        ),
    )(*operands)
    return basis, remainder, entries.T


def solution(mesh):
    return jax.shard_map(
        functools.partial(shards, mesh.shape["rows"], mesh.shape["grp"]),
        mesh=mesh,
        in_specs=(
            P(("rows", "grp"), None, None),
            P(("rows", "grp"), None),
            P(("rows", "grp"), None, None, None),
            P(("rows", "grp"), None, None),
            P(("rows", "grp"), None, None),
            P(("rows", "grp"), None),
            P(("rows", "grp"), None, None),
            P(("rows", "grp"), None, None),
            P(("rows", "grp"), None),
            P(("rows", "grp"), None, None),
            P(("rows", "grp"), None, None),
            P("rows", None),
            P("rows", None, None),
        ),
        out_specs=(P(("rows", "grp"), None, None), P(("rows", "grp"), None, None), P()),
        check_vma=False,
    )
```

time: 400 us -> 35.3 us (0.09); the launches traced: 395 us -> 35.1 us
  blocking collectives: 261 us -> 0 us
  local copies, waits for them, and re-layouts: 63.9 us -> 4.34 us
  other arithmetic: 35.6 us -> 0 us
  Pallas kernels: 0 us -> 30.1 us
  matrix products: 24.3 us -> 0 us
  starting transfers between devices: 9.28 us -> 0 us
    all_gather x2 -> x0, blocking collectives: 136 us -> none  [apply_operator(): gathered = lax.all_gather(packed, ('rows', 'grp'), axis=0, tiled=True)]
    psum x3 -> x0, blocking collectives: 125 us -> none  [stacked_means(): return lax.psum(partial_sums, ('rows', 'grp')) / total_count]
    pallas_call x0 -> x1, Pallas kernels: none -> 30.1 us  [shards(): pl.pallas_call(functools.partial(kernel, rows, grp), out_shape=(jax.Shape...]
    dot_general x20 -> x0, matrix products: 24.3 us -> none  [the longest x2 4.19 us: apply_operator(): jnp.einsum('lkbj,lkij->lbi', picked, near_blocks, preferred_element_type=...]
    reshape x20 -> x0, local copies, waits for them, and re-layouts: 23.4 us -> none  [the longest x10 11.2 us: pick_flat(): chosen = chosen.reshape(target_count, slot_count, -1, R)]
    gather x8 -> x0, local copies, waits for them, and re-layouts: 15 us -> none  [the longest x6 10.5 us: pick_flat(): chosen = jnp.take(source, indices, axis=0)]
    select_n x7 -> x0, other arithmetic: 9.48 us -> none  [pick_flat(): chosen = jnp.take(source, indices, axis=0)]
    ppermute x4 -> x0, starting transfers between devices: 9.28 us -> none  [the longest x2 6.72 us: padded(): lax.ppermute(lax.slice_in_dim(block, block.shape[dim] - width, None, axis...]
  transfers between devices with their start and end apart: 4 -> 0, of which waited for: 0 -> 0; matrix products, arithmetic and copies ran while one was open for 22% -> 0% of each run, Pallas kernels for 0% -> 0%
where the time goes in v1:
time: 35.3 us; the launch traced here: 35.1 us
  Pallas kernels  30.1 us (85%)
  local copies, waits for them, and re-layouts  4.34 us (12%)
  between operations  0.64 us (2%)
    pallas_call x1, Pallas kernels, shards(): pl.pallas_call(functools.partial(kernel, rows, grp), out_shape=(jax.Shape...  30.1 us
    unnamed x3, local copies, waits for them, and re-layouts  4.34 us

profile of v1, /device:TPU:0, one launch (start us, length us, event | category | flops | bytes accessed | tf_op | source)
XLA Modules:
  0.0 35.1 jit_solution(455643371212810443)
XLA Ops:
  0.6 30.1 %shard_map.148 = (f32[4,16,384]{2,1,0:T(8,128)}, f32[4,16,384]{2,1,0:T(8,128)}, f32[5,16]{1,0:T(8,128)}) custom-call(s32[4,3]{1,0:T(4,128)} %refs_0_.1, s32[4,8]{1,0:T(4,128)} %refs_1_.1, s32[1,4]{1,0:T(1,128)} %refs_2_.1, s32[1,4]{1,0:T(1,128)} %refs_3_.1, f32[4,16,384]{2,1,0:T(8,128)} %refs_4_.1, bf16[4,3,384,384]{3,2,1,0:T(8,128)(2,1)} %refs_5_.1, ...), custom_call_target="tpu_custom_call" | custom-call | tf_op jit(solution)/shard_map/pallas_call | solution.py:506
  30.7 1.5 %copy.19 = f32[4,16,384]{2,1,0:T(8,128)} copy(f32[4,16,384]{2,1,0:T(8,128)} %get-tuple-element.12) | data formatting | bytes 196608
  32.3 1.5 %copy.20 = f32[4,16,384]{2,1,0:T(8,128)} copy(f32[4,16,384]{2,1,0:T(8,128)} %get-tuple-element.13) | data formatting | bytes 196608
  33.8 1.3 %copy.21 = f32[16,5]{0,1:T(8,128)} copy(f32[16,5]{0,1:T(8,128)} %bitcast.1) | data formatting | bytes 640

commit v2 on v1

--- a/solution.py
+++ b/solution.py
@@ -21,14 +21,8 @@
     )
 
 
-def spread_matrix(rows, slots, rank, low, copies):
-    shape = (rows, slots * LANES)
-    row = lax.broadcasted_iota(jnp.int32, shape, 0)
-    column = lax.broadcasted_iota(jnp.int32, shape, 1)
-    lane = column % LANES - low
-    wanted = (column // LANES) * rank + lane % rank
-    hit = (row == wanted) & (lane >= 0) & (lane < copies * rank)
-    return jnp.where(hit, 1.0, 0.0).astype(bf16)
+def wrap(index, size):
+    return jnp.where(index >= size, index - size, index)
 
 
 def kernel(
@@ -37,7 +31,7 @@
     *refs,
 ):
     sources = refs[:13]
-    basis_out, remainder_out, hessenberg_out = refs[13:16]
+    results = refs[13:16]
     targets = refs[16:29]
     (
         near_cols,
@@ -70,6 +64,11 @@
         group_weights,
         image,
         image_two,
+        select,
+        basis_out,
+        remainder_out,
+        hessenberg_out,
+        store_sem,
         load_sem,
         field_send,
         field_recv,
@@ -101,17 +100,21 @@
 
     barrier = pltpu.get_barrier_semaphore()
 
-    def greet(step, carry):
-        other = lax.rem(me + step, devices)
-        pl.semaphore_signal(
-            barrier,
-            inc=1,
-            device_id=(lax.div(other, grp), lax.rem(other, grp)),
-            device_id_type=MESH,
-        )
-        return carry
-
-    lax.fori_loop(1, devices, greet, 0)
+    def each_other(visit):
+        def one_row(step, carry):
+            to_row = wrap(row + step, rows)
+            for turn in range(grp):
+                visit(to_row, wrap(z + turn, grp))
+            return carry
+
+        for turn in range(1, grp):
+            visit(row, wrap(z + turn, grp))
+        lax.fori_loop(1, rows, one_row, 0)
+
+    def greet(to_row, to_z):
+        pl.semaphore_signal(barrier, inc=1, device_id=(to_row, to_z), device_id_type=MESH)
+
+    each_other(greet)
 
     send_basis[...] = jnp.zeros_like(send_basis)
     for n in (4, 6, 9, 11):
@@ -120,22 +123,15 @@
         send_basis[l * rank : (l + 1) * rank, l * cells : (l + 1) * cells] = col_basis[l]
     width = leaves * rank
     transfer = leaf_transfer[...].reshape(width, rank)
-    up_box = lax.dot_general(
-        transfer,
-        send_basis[:width].astype(f32),
-        (((0,), (0,)), ((), ())),
-        precision=highest,
-        preferred_element_type=f32,
-    )
-    up_parent = lax.dot_general(
-        box_transfer[0],
-        up_box,
-        (((0,), (0,)), ((), ())),
-        precision=highest,
-        preferred_element_type=f32,
-    )
-    send_basis[width : width + rank] = up_box.astype(bf16)
-    send_basis[width + rank : width + 2 * rank] = up_parent.astype(bf16)
+    down = jnp.dot(transfer, box_transfer[0], precision=highest, preferred_element_type=f32)
+    up = jnp.concatenate([transfer, down], axis=1).T
+    up_high = up.astype(bf16)
+    up_low = (up - up_high.astype(f32)).astype(bf16)
+    plain = send_basis[:width]
+    send_basis[width : width + 2 * rank] = (
+        jnp.dot(up_high, plain, preferred_element_type=f32)
+        + jnp.dot(up_low, plain, preferred_element_type=f32)
+    ).astype(bf16)
 
     def prepare_receive():
         for n in (7, 8, 10, 12, 0, 1, 2, 3):
@@ -143,36 +139,42 @@
         receive_basis[...] = jnp.zeros_like(receive_basis)
         for l in range(leaves):
             receive_basis[l * rank : (l + 1) * rank, l * cells : (l + 1) * cells] = row_basis[l]
+        lane = lax.broadcasted_iota(jnp.int32, (rank, LANES), 1)
+        unit = lax.broadcasted_iota(jnp.int32, (rank, LANES), 0)
+        select[...] = jnp.zeros_like(select)
+        for k in range(select.shape[0] // rank):
+            select[k * rank : (k + 1) * rank, k * LANES : (k + 1) * LANES] = jnp.where(
+                (lane & (rank - 1)) == unit, 1.0, 0.0
+            ).astype(bf16)
         tiled = jnp.dot(
             leaf_coupling[...].reshape(width, leaf_slots * rank),
-            spread_matrix(leaf_slots * rank, leaf_slots, rank, 0, leaves),
+            select[: leaf_slots * rank, : leaf_slots * LANES],
             preferred_element_type=f32,
         )
-        part = lax.broadcasted_iota(jnp.int32, (rank, LANES), 1) // rank
         for l in range(leaves):
             for k in range(leaf_slots):
-                sub = lax.rem(leaf_far[l, k], leaves)
+                start = lax.rem(leaf_far[l, k], leaves) * rank
                 piece = tiled[l * rank : (l + 1) * rank, k * LANES : (k + 1) * LANES]
                 leaf_weights[l, :, k * LANES : (k + 1) * LANES] = jnp.where(
-                    part == sub, piece, 0.0
+                    (lane >= start) & (lane < start + rank), piece, 0.0
                 ).astype(bf16)
-        box_wide = jnp.dot(
-            box_coupling[0],
-            spread_matrix(box_slots * rank, box_slots, rank, 0, 1),
-            preferred_element_type=f32,
-        )
-        box_weights[...] = jnp.dot(
-            transfer, box_wide, precision=highest, preferred_element_type=f32
-        ).astype(bf16)
-        group_wide = jnp.dot(
-            coarse_coupling[0],
-            spread_matrix(coarse_slots * rank, coarse_slots, rank, rank, 1),
-            preferred_element_type=f32,
-        )
-        down = jnp.dot(transfer, box_transfer[0], precision=highest, preferred_element_type=f32)
-        group_weights[...] = jnp.dot(
-            down, group_wide, precision=highest, preferred_element_type=f32
-        ).astype(bf16)
+
+        def compose(target, coupling, above, low):
+            slots = coupling.shape[1] // rank
+            wide = jnp.dot(
+                coupling, select[: slots * rank, : slots * LANES], preferred_element_type=f32
+            )
+            place = lax.broadcasted_iota(jnp.int32, wide.shape, 1) & (LANES - 1)
+            wide = jnp.where((place >= low) & (place < low + rank), wide, 0.0).astype(bf16)
+            above_high = above.astype(bf16)
+            above_low = (above - above_high.astype(f32)).astype(bf16)
+            target[...] = (
+                jnp.dot(above_high, wide, preferred_element_type=f32)
+                + jnp.dot(above_low, wide, preferred_element_type=f32)
+            ).astype(bf16)
+
+        compose(box_weights, box_coupling[0], transfer, 0)
+        compose(group_weights, coarse_coupling[0], down, rank)
 
     def send(src, dst, send_sem, recv_sem, to_row, to_z):
         pltpu.make_async_remote_copy(
@@ -198,26 +200,25 @@
 
         @pl.when(me < devices - 1)
         def _():
-            other = me + 1
+            last = z == grp - 1
             send(
                 own,
                 low,
                 field_send.at[phase, 0],
                 field_recv.at[phase, 0],
-                lax.div(other, grp),
-                lax.rem(other, grp),
+                jnp.where(last, row + 1, row),
+                jnp.where(last, 0, z + 1),
             )
 
         @pl.when(me > 0)
         def _():
-            other = me - 1
             send(
                 own,
                 high,
                 field_send.at[phase, 1],
                 field_recv.at[phase, 1],
-                lax.div(other, grp),
-                lax.rem(other, grp),
+                jnp.where(z == 0, row - 1, row),
+                jnp.where(z == 0, grp - 1, z - 1),
             )
 
         wide = jnp.concatenate([field[leaves + l] for l in range(leaves)], axis=1)
@@ -233,7 +234,7 @@
                 coef_send.at[phase, 1],
                 coef_recv.at[phase, 1],
                 row,
-                lax.rem(z + step, grp),
+                wrap(z + step, grp),
             )
 
         @pl.when(row > 0)
@@ -278,7 +279,7 @@
                 group.at[row],
                 group_send.at[phase],
                 group_recv.at[phase],
-                lax.rem(row + step, rows),
+                wrap(row + step, rows),
                 z,
             )
             return carry
@@ -369,19 +370,17 @@
             spread = jnp.where(lane_at == sub_at + n * rhs, column, spread)
         sums[me] = jnp.sum(spread, axis=0, keepdims=True)
 
-        def send_sums(step, carry):
-            other = lax.rem(me + step, devices)
+        def send_sums(to_row, to_z):
             send(
                 sums.at[me],
                 sums.at[me],
                 sums_send.at[index],
                 sums_recv.at[index],
-                lax.div(other, grp),
-                lax.rem(other, grp),
+                to_row,
+                to_z,
             )
-            return carry
-
-        lax.fori_loop(1, devices, send_sums, 0)
+
+        each_other(send_sums)
 
     def finish_sums(index, sums, count):
         wait_bytes(sums.at[pl.ds(0, devices - 1)], sums_recv.at[index])
@@ -420,6 +419,12 @@
     image_square = (uu + 2.0 * shift * vu + shift * shift * vv) * scale_first * scale_first
     norm_image = jnp.sqrt(jnp.maximum(image_square, 0.0) + epsilon)
     scale = scale_first / norm_image
+    stores = [
+        pltpu.make_async_copy(source, result, store_sem.at[n])
+        for n, (source, result) in enumerate(
+            zip((basis_out, remainder_out, hessenberg_out), results)
+        )
+    ]
     for l in range(leaves):
         basis = (image[l] + shift * vector[l]) * scale
         basis_out[l] = basis
@@ -437,6 +442,7 @@
             ]
         ),
     )
+    stores[0].start()
     drain(0, field_a, coef_a, group_a)
     drain(1, field_b, coef_b, group_b)
     wait_bytes(sums_a.at[pl.ds(0, devices - 1)], sums_send.at[0])
@@ -449,6 +455,7 @@
         remainder_out[l] = (
             remainder_out[l] - first_part * vector[l] - proj_basis * basis_out[l]
         )
+    stores[1].start()
     last_square = (
         square_two
         + first_with * first_with * first_square
@@ -461,7 +468,20 @@
     for n, entry in enumerate([proj_first, norm_image, first_with, proj_basis, norm_last]):
         line = jnp.sum(jnp.where(lane_at == sub_at, entry, 0.0), axis=0, keepdims=True)
         hessenberg_out[n : n + 1, :] = line[:, :rhs]
+    stores[2].start()
     wait_bytes(sums_b.at[pl.ds(0, devices - 1)], sums_send.at[1])
+    for store in stores:
+        store.wait()
+
+
+def hand_on(*refs):
+    copies = [
+        pltpu.make_async_copy(refs[n], refs[3 + n], refs[6].at[n]) for n in range(3)
+    ]
+    for copy in copies:
+        copy.start()
+    for copy in copies:
+        copy.wait()
 
 
 def shards(
@@ -485,8 +505,9 @@
     rank = col_basis.shape[1]
     devices = rows * grp
     assert leaves * rank == LANES and box_far.shape[0] == 1 and coarse_far.shape[0] == 1
-    assert 5 * rhs <= LANES
-    vmem = pl.BlockSpec(memory_space=pltpu.VMEM)
+    assert 5 * rhs <= LANES and rank & (rank - 1) == 0
+    hbm = pl.BlockSpec(memory_space=pltpu.HBM)
+    slots = max(leaf_far.shape[1], box_far.shape[1], coarse_far.shape[1])
     dma = pltpu.SemaphoreType.DMA
     operands = (
         near_cols,
@@ -503,15 +524,16 @@
         box_transfer,
         coarse_coupling,
     )
-    basis, remainder, entries = pl.pallas_call(
+    shapes = (
+        jax.ShapeDtypeStruct(vector.shape, f32),
+        jax.ShapeDtypeStruct(vector.shape, f32),
+        jax.ShapeDtypeStruct((5, rhs), f32),
+    )
+    results = pl.pallas_call(
         functools.partial(kernel, rows, grp),
-        out_shape=(
-            jax.ShapeDtypeStruct(vector.shape, f32),
-            jax.ShapeDtypeStruct(vector.shape, f32),
-            jax.ShapeDtypeStruct((5, rhs), f32),
-        ),
-        in_specs=[pl.BlockSpec(memory_space=pltpu.HBM)] * len(operands),
-        out_specs=(vmem, vmem, vmem),
+        out_shape=shapes,
+        in_specs=[hbm] * len(operands),
+        out_specs=(hbm, hbm, hbm),
         scratch_shapes=[
             *[pltpu.SMEM(operand.shape, operand.dtype) for operand in operands[:4]],
             *[pltpu.VMEM(operand.shape, operand.dtype) for operand in operands[4:]],
@@ -530,6 +552,11 @@
             pltpu.VMEM((LANES, coarse_far.shape[1] * LANES), bf16),
             pltpu.VMEM(vector.shape, f32),
             pltpu.VMEM(vector.shape, f32),
+            pltpu.VMEM((slots * rank, slots * LANES), bf16),
+            pltpu.VMEM(vector.shape, f32),
+            pltpu.VMEM(vector.shape, f32),
+            pltpu.VMEM((5, rhs), f32),
+            dma((3,)),
             dma((len(operands),)),
             dma((2, 2)),
             dma((2, 2)),
@@ -544,6 +571,14 @@
             collective_id=0, has_side_effects=True, vmem_limit_bytes=65100 * 1024
         ),
     )(*operands)
+    basis, remainder, entries = pl.pallas_call(
+        hand_on,
+        out_shape=shapes,
+        in_specs=[hbm] * 3,
+        out_specs=(hbm, hbm, hbm),
+        scratch_shapes=[dma((3,))],
+        compiler_params=pltpu.CompilerParams(vmem_limit_bytes=65100 * 1024),
+    )(*results)
     return basis, remainder, entries.T
 
 

time: 35.3 us -> 38.1 us (1.079)
  Pallas kernels: 30.1 us -> 37.3 us
  local copies, waits for them, and re-layouts: 4.34 us -> 0 us
    pallas_call x1 -> x2, Pallas kernels: 30.1 us -> 37.3 us  [the longest x1 30.2 us: shards(): pl.pallas_call(functools.partial(kernel, rows, grp), out_shape=shapes, in...]
    unnamed x3 -> x0, local copies, waits for them, and re-layouts: 4.34 us -> none
where the time goes in v2:
time: 38.1 us; the launch traced here: 38 us
  Pallas kernels  37.3 us (98%)
  between operations  0.64 us (2%)
    pallas_call x1, Pallas kernels, shards(): pl.pallas_call(functools.partial(kernel, rows, grp), out_shape=shapes, in...  30.2 us
    pallas_call x1, Pallas kernels, shards(): pl.pallas_call(hand_on, out_shape=shapes, in_specs=[hbm] * 3, out_specs=(...  7.16 us

profile of v2, /device:TPU:0, one launch (start us, length us, event | category | flops | bytes accessed | tf_op | source)
XLA Modules:
  0.0 38.0 jit_solution(7621886705766761581)
XLA Ops:
  0.6 30.2 %shard_map.148 = (f32[4,16,384]{2,1,0:T(8,128)}, f32[4,16,384]{2,1,0:T(8,128)}, f32[5,16]{1,0:T(8,128)}) custom-call(s32[4,3]{1,0:T(4,128)} %refs_0_.1, s32[4,8]{1,0:T(4,128)} %refs_1_.1, s32[1,4]{1,0:T(1,128)} %refs_2_.1, s32[1,4]{1,0:T(1,128)} %refs_3_.1, f32[4,16,384]{2,1,0:T(8,128)} %refs_4_.1, bf16[4,3,384,384]{3,2,1,0:T(8,128)(2,1)} %refs_5_.1, ...), custom_call_target="tpu_custom_call" | custom-call | tf_op jit(solution)/shard_map/pallas_call | solution.py:532
  30.8 7.2 %shard_map.149 = (f32[4,16,384]{2,1,0:T(8,128)}, f32[4,16,384]{2,1,0:T(8,128)}, f32[5,16]{1,0:T(8,128)}) custom-call(f32[4,16,384]{2,1,0:T(8,128)} %get-tuple-element.9.refs_0_, f32[4,16,384]{2,1,0:T(8,128)} %get-tuple-element.10.refs_1_, f32[5,16]{1,0:T(8,128)} %get-tuple-element.11.refs_2_), custom_call_target="tpu_custom_call" | custom-call | tf_op jit(solution)/shard_map/pallas_call | solution.py:574

commit v3 on v2

--- a/solution.py
+++ b/solution.py
@@ -100,21 +100,28 @@
 
     barrier = pltpu.get_barrier_semaphore()
 
-    def each_other(visit):
-        def one_row(step, carry):
-            to_row = wrap(row + step, rows)
-            for turn in range(grp):
-                visit(to_row, wrap(z + turn, grp))
-            return carry
-
-        for turn in range(1, grp):
-            visit(row, wrap(z + turn, grp))
-        lax.fori_loop(1, rows, one_row, 0)
-
     def greet(to_row, to_z):
         pl.semaphore_signal(barrier, inc=1, device_id=(to_row, to_z), device_id_type=MESH)
 
-    each_other(greet)
+    def greet_row(step, carry):
+        greet(wrap(row + step, rows), z)
+        return carry
+
+    for turn in range(1, grp):
+        other = wrap(z + turn, grp)
+        greet(row, other)
+
+        @pl.when(row > 0)
+        def _():
+            greet(row - 1, other)
+
+        @pl.when(row < rows - 1)
+        def _():
+            greet(row + 1, other)
+
+    lax.fori_loop(1, rows, greet_row, 0)
+    beside = jnp.where(row > 0, 1, 0) + jnp.where(row < rows - 1, 1, 0)
+    greetings = (grp - 1) * (1 + beside) + rows - 1
 
     send_basis[...] = jnp.zeros_like(send_basis)
     for n in (4, 6, 9, 11):
@@ -189,11 +196,34 @@
     def wait_bytes(ref, sem):
         pltpu.make_async_copy(ref, ref, sem).wait()
 
-    def operator(phase, source, result, field, coef, group, after_send, before_near):
+    sub_at = lax.broadcasted_iota(jnp.int32, (rhs, LANES), 0)
+    lane_at = lax.broadcasted_iota(jnp.int32, (rhs, LANES), 1)
+
+    def with_sums(tile, columns):
+        for n, column in enumerate(columns):
+            for part in range(3):
+                piece = column.astype(bf16).astype(f32)
+                tile = jnp.where(lane_at == 2 * rank + 3 * n + part, piece, tile)
+                column = column - piece
+        return tile
+
+    def read_sums(tile, count):
+        return [
+            jnp.sum(
+                jnp.where(
+                    (lane_at >= 2 * rank + 3 * n) & (lane_at < 2 * rank + 3 * n + 3), tile, 0.0
+                ),
+                axis=1,
+                keepdims=True,
+            )
+            for n in range(count)
+        ]
+
+    def operator(phase, source, result, field, coef, group, sums, after_send, before_near):
         for l in range(leaves):
             field[leaves + l] = source[l].astype(bf16)
         if phase == 0:
-            pl.semaphore_wait(barrier, devices - 1)
+            pl.semaphore_wait(barrier, greetings)
         own = field.at[pl.ds(leaves, leaves)]
         low = field.at[pl.ds(0, leaves)]
         high = field.at[pl.ds(2 * leaves, leaves)]
@@ -222,10 +252,10 @@
             )
 
         wide = jnp.concatenate([field[leaves + l] for l in range(leaves)], axis=1)
-        sent = nt(wide, send_basis[...]).astype(bf16)
+        sent = nt(wide, send_basis[...])
         mine = grp + z
-        coef[mine, 0] = sent[:, :LANES]
-        coef[mine, 1] = sent[:, LANES:]
+        coef[mine, 0] = sent[:, :LANES].astype(bf16)
+        coef[mine, 1] = with_sums(sent[:, LANES:], sums()).astype(bf16)
 
         for step in range(1, grp):
             send(
@@ -271,6 +301,8 @@
         together = coef[grp, 1].astype(f32)
         for other in range(1, grp):
             together = together + coef[grp + other, 1].astype(f32)
+        if phase == 1:
+            together = with_sums(together, read_sums(together, 3))
         group[row] = together.astype(bf16)
 
         def send_group(step, carry):
@@ -360,31 +392,41 @@
         if rows > 1:
             wait_bytes(group.at[pl.ds(0, rows - 1)], group_send.at[phase])
 
-    sub_at = lax.broadcasted_iota(jnp.int32, (rhs, LANES), 0)
-    lane_at = lax.broadcasted_iota(jnp.int32, (rhs, LANES), 1)
-
-    def start_sums(index, sums, products):
+    def start_sums(columns):
         spread = jnp.zeros((rhs, LANES), f32)
-        for n, product in enumerate(products):
-            column = jnp.sum(product, axis=1, keepdims=True)
+        for n, column in enumerate(columns):
             spread = jnp.where(lane_at == sub_at + n * rhs, column, spread)
-        sums[me] = jnp.sum(spread, axis=0, keepdims=True)
-
-        def send_sums(to_row, to_z):
+        sums_a[z] = jnp.sum(spread, axis=0, keepdims=True)
+        for turn in range(1, grp):
             send(
-                sums.at[me],
-                sums.at[me],
-                sums_send.at[index],
-                sums_recv.at[index],
-                to_row,
-                to_z,
-            )
-
-        each_other(send_sums)
-
-    def finish_sums(index, sums, count):
-        wait_bytes(sums.at[pl.ds(0, devices - 1)], sums_recv.at[index])
-        line = jnp.sum(sums[...], axis=0) / total_count
+                sums_a.at[z],
+                sums_a.at[z],
+                sums_send.at[0],
+                sums_recv.at[0],
+                row,
+                wrap(z + turn, grp),
+            )
+
+    def finish_sums(count):
+        if grp > 1:
+            wait_bytes(sums_a.at[pl.ds(0, grp - 1)], sums_recv.at[0])
+        sums_b[row] = jnp.sum(sums_a[...], axis=0)
+
+        def send_sums(step, carry):
+            send(
+                sums_b.at[row],
+                sums_b.at[row],
+                sums_send.at[1],
+                sums_recv.at[1],
+                wrap(row + step, rows),
+                z,
+            )
+            return carry
+
+        lax.fori_loop(1, rows, send_sums, 0)
+        if rows > 1:
+            wait_bytes(sums_b.at[pl.ds(0, rows - 1)], sums_recv.at[1])
+        line = jnp.sum(sums_b[...], axis=0) / total_count
         spread = jnp.broadcast_to(line, (rhs, LANES))
         return [
             jnp.sum(jnp.where(lane_at == sub_at + n * rhs, spread, 0.0), axis=1, keepdims=True)
@@ -397,20 +439,39 @@
             total = left[0] * right[0]
             for l in range(1, leaves):
                 total = total + left[l] * right[l]
-            sums.append(total)
+            sums.append(jnp.sum(total, axis=1, keepdims=True))
         return sums
 
-    def start_first_sums():
-        start_sums(
-            0, sums_a, products([(vector, vector), (vector, image), (image, image)])
-        )
-
-    operator(0, vector, image, field_a, coef_a, group_a, prepare_receive, loads[5].wait)
+    def first_sums():
+        return products([(vector, vector), (vector, image), (image, image)])
+
     operator(
-        1, image, image_two, field_b, coef_b, group_b, start_first_sums, lambda: None
-    )
-
-    vv, vu, uu = finish_sums(0, sums_a, 3)
+        0,
+        vector,
+        image,
+        field_a,
+        coef_a,
+        group_a,
+        lambda: [],
+        prepare_receive,
+        loads[5].wait,
+    )
+    operator(
+        1,
+        image,
+        image_two,
+        field_b,
+        coef_b,
+        group_b,
+        first_sums,
+        lambda: None,
+        lambda: None,
+    )
+
+    together = group_b[0].astype(f32)
+    for n in range(1, rows):
+        together = together + group_b[n].astype(f32)
+    vv, vu, uu = [column / total_count for column in read_sums(together, 3)]
     norm_first = jnp.sqrt(vv + epsilon)
     scale_first = 1.0 / norm_first
     first_square = vv * scale_first * scale_first
@@ -430,8 +491,6 @@
         basis_out[l] = basis
         remainder_out[l] = 0.5 * basis + (image_two[l] + shift * image[l]) * scale
     start_sums(
-        1,
-        sums_b,
         products(
             [
                 (vector, remainder_out),
@@ -440,13 +499,11 @@
                 (basis_out, vector),
                 (basis_out, basis_out),
             ]
-        ),
+        )
     )
     stores[0].start()
     drain(0, field_a, coef_a, group_a)
-    drain(1, field_b, coef_b, group_b)
-    wait_bytes(sums_a.at[pl.ds(0, devices - 1)], sums_send.at[0])
-    first_with, basis_with, square_two, cross_term, basis_square = finish_sums(1, sums_b, 5)
+    first_with, basis_with, square_two, cross_term, basis_square = finish_sums(5)
     first_with = first_with * scale_first
     cross_term = cross_term * scale_first
     proj_basis = basis_with - first_with * cross_term
@@ -469,19 +526,26 @@
         line = jnp.sum(jnp.where(lane_at == sub_at, entry, 0.0), axis=0, keepdims=True)
         hessenberg_out[n : n + 1, :] = line[:, :rhs]
     stores[2].start()
-    wait_bytes(sums_b.at[pl.ds(0, devices - 1)], sums_send.at[1])
+    drain(1, field_b, coef_b, group_b)
+    if grp > 1:
+        wait_bytes(sums_a.at[pl.ds(0, grp - 1)], sums_send.at[0])
+    if rows > 1:
+        wait_bytes(sums_b.at[pl.ds(0, rows - 1)], sums_send.at[1])
     for store in stores:
         store.wait()
 
 
 def hand_on(*refs):
-    copies = [
-        pltpu.make_async_copy(refs[n], refs[3 + n], refs[6].at[n]) for n in range(3)
-    ]
-    for copy in copies:
-        copy.start()
-    for copy in copies:
-        copy.wait()
+    sources, results, places, load_sem, store_sem = refs[:3], refs[3:6], refs[6:9], refs[9], refs[10]
+    loads = [pltpu.make_async_copy(sources[n], places[n], load_sem.at[n]) for n in range(3)]
+    stores = [pltpu.make_async_copy(places[n], results[n], store_sem.at[n]) for n in range(3)]
+    for load in loads:
+        load.start()
+    for load, store in zip(loads, stores):
+        load.wait()
+        store.start()
+    for store in stores:
+        store.wait()
 
 
 def shards(
@@ -503,9 +567,8 @@
 ):
     leaves, rhs, cells = vector.shape
     rank = col_basis.shape[1]
-    devices = rows * grp
     assert leaves * rank == LANES and box_far.shape[0] == 1 and coarse_far.shape[0] == 1
-    assert 5 * rhs <= LANES and rank & (rank - 1) == 0
+    assert 5 * rhs <= LANES and 2 * rank + 9 <= LANES and rank & (rank - 1) == 0
     hbm = pl.BlockSpec(memory_space=pltpu.HBM)
     slots = max(leaf_far.shape[1], box_far.shape[1], coarse_far.shape[1])
     dma = pltpu.SemaphoreType.DMA
@@ -543,8 +606,8 @@
             pltpu.VMEM((3 * grp, 2, rhs, LANES), bf16),
             pltpu.VMEM((rows, rhs, LANES), bf16),
             pltpu.VMEM((rows, rhs, LANES), bf16),
-            pltpu.VMEM((devices, 1, LANES), f32),
-            pltpu.VMEM((devices, 1, LANES), f32),
+            pltpu.VMEM((grp, 1, LANES), f32),
+            pltpu.VMEM((rows, 1, LANES), f32),
             pltpu.VMEM((2 * LANES, leaves * cells), bf16),
             pltpu.VMEM((LANES, leaves * cells), bf16),
             pltpu.VMEM((leaves, rank, leaf_far.shape[1] * LANES), bf16),
@@ -576,7 +639,7 @@
         out_shape=shapes,
         in_specs=[hbm] * 3,
         out_specs=(hbm, hbm, hbm),
-        scratch_shapes=[dma((3,))],
+        scratch_shapes=[pltpu.VMEM(shape.shape, f32) for shape in shapes] + [dma((3,))] * 2,
         compiler_params=pltpu.CompilerParams(vmem_limit_bytes=65100 * 1024),
     )(*results)
     return basis, remainder, entries.T

time: 38.1 us -> 33.7 us (0.88)
  Pallas kernels: 37.3 us -> 32.9 us
    pallas_call x1, Pallas kernels: 7.16 us -> 1.63 us  [shards(): pl.pallas_call(hand_on, out_shape=shapes, in_specs=[hbm] * 3, out_specs=(...]
    pallas_call x1, Pallas kernels: 30.2 us -> 31.3 us  [shards(): pl.pallas_call(functools.partial(kernel, rows, grp), out_shape=shapes, in...]
where the time goes in v3:
time: 33.7 us; the launch traced here: 33.5 us
  Pallas kernels  32.9 us (98%)
  between operations  0.64 us (2%)
    pallas_call x1, Pallas kernels, shards(): pl.pallas_call(functools.partial(kernel, rows, grp), out_shape=shapes, in...  31.3 us
    pallas_call x1, Pallas kernels, shards(): pl.pallas_call(hand_on, out_shape=shapes, in_specs=[hbm] * 3, out_specs=(...  1.63 us

profile of v3, /device:TPU:0, one launch (start us, length us, event | category | flops | bytes accessed | tf_op | source)
XLA Modules:
  0.0 33.5 jit_solution(14516440873746833342)
XLA Ops:
  0.6 31.3 %shard_map.148 = (f32[4,16,384]{2,1,0:T(8,128)}, f32[4,16,384]{2,1,0:T(8,128)}, f32[5,16]{1,0:T(8,128)}) custom-call(s32[4,3]{1,0:T(4,128)} %refs_0_.1, s32[4,8]{1,0:T(4,128)} %refs_1_.1, s32[1,4]{1,0:T(1,128)} %refs_2_.1, s32[1,4]{1,0:T(1,128)} %refs_3_.1, f32[4,16,384]{2,1,0:T(8,128)} %refs_4_.1, bf16[4,3,384,384]{3,2,1,0:T(8,128)(2,1)} %refs_5_.1, ...), custom_call_target="tpu_custom_call" | custom-call | tf_op jit(solution)/shard_map/pallas_call | solution.py:595
  31.9 1.6 %shard_map.149 = (f32[4,16,384]{2,1,0:T(8,128)}, f32[4,16,384]{2,1,0:T(8,128)}, f32[5,16]{1,0:T(8,128)}) custom-call(f32[4,16,384]{2,1,0:T(8,128)} %get-tuple-element.9.refs_0_, f32[4,16,384]{2,1,0:T(8,128)} %get-tuple-element.10.refs_1_, f32[5,16]{1,0:T(8,128)} %get-tuple-element.11.refs_2_), custom_call_target="tpu_custom_call" | custom-call | tf_op jit(solution)/shard_map/pallas_call | solution.py:637

commit v4 on v3

--- a/solution.py
+++ b/solution.py
@@ -55,8 +55,7 @@
         coef_b,
         group_a,
         group_b,
-        sums_a,
-        sums_b,
+        sums,
         send_basis,
         receive_basis,
         leaf_weights,
@@ -64,6 +63,7 @@
         group_weights,
         image,
         image_two,
+        picked,
         select,
         basis_out,
         remainder_out,
@@ -100,30 +100,24 @@
 
     barrier = pltpu.get_barrier_semaphore()
 
+    def each_other(visit):
+        def one_row(step, carry):
+            to_row = wrap(row + step, rows)
+            for turn in range(grp):
+                visit(to_row, wrap(z + turn, grp))
+            return carry
+
+        for turn in range(1, grp):
+            visit(row, wrap(z + turn, grp))
+        lax.fori_loop(1, rows, one_row, 0)
+
     def greet(to_row, to_z):
         pl.semaphore_signal(barrier, inc=1, device_id=(to_row, to_z), device_id_type=MESH)
 
-    def greet_row(step, carry):
-        greet(wrap(row + step, rows), z)
-        return carry
-
-    for turn in range(1, grp):
-        other = wrap(z + turn, grp)
-        greet(row, other)
-
-        @pl.when(row > 0)
-        def _():
-            greet(row - 1, other)
-
-        @pl.when(row < rows - 1)
-        def _():
-            greet(row + 1, other)
-
-    lax.fori_loop(1, rows, greet_row, 0)
-    beside = jnp.where(row > 0, 1, 0) + jnp.where(row < rows - 1, 1, 0)
-    greetings = (grp - 1) * (1 + beside) + rows - 1
+    each_other(greet)
 
     send_basis[...] = jnp.zeros_like(send_basis)
+    picked[...] = jnp.zeros_like(picked)
     for n in (4, 6, 9, 11):
         loads[n].wait()
     for l in range(leaves):
@@ -196,6 +190,18 @@
     def wait_bytes(ref, sem):
         pltpu.make_async_copy(ref, ref, sem).wait()
 
+    def near_product(result, start, stop, pick, add):
+        total = None
+        for l in range(leaves):
+            for k in range(start, stop):
+                picked[l, k, l * rhs : (l + 1) * rhs] = pick(l, k)
+                product = nt(near_blocks[l, k], picked[l, k])
+                total = product if total is None else total + product
+        turned = total.T
+        for l in range(leaves):
+            rows_of = turned[l * rhs : (l + 1) * rhs]
+            result[l] = result[l] + rows_of if add else rows_of
+
     sub_at = lax.broadcasted_iota(jnp.int32, (rhs, LANES), 0)
     lane_at = lax.broadcasted_iota(jnp.int32, (rhs, LANES), 1)
 
@@ -219,11 +225,11 @@
             for n in range(count)
         ]
 
-    def operator(phase, source, result, field, coef, group, sums, after_send, before_near):
+    def operator(phase, source, result, field, coef, group, own_sums, after_send, before_near):
         for l in range(leaves):
             field[leaves + l] = source[l].astype(bf16)
         if phase == 0:
-            pl.semaphore_wait(barrier, greetings)
+            pl.semaphore_wait(barrier, devices - 1)
         own = field.at[pl.ds(leaves, leaves)]
         low = field.at[pl.ds(0, leaves)]
         high = field.at[pl.ds(2 * leaves, leaves)]
@@ -255,7 +261,7 @@
         sent = nt(wide, send_basis[...])
         mine = grp + z
         coef[mine, 0] = sent[:, :LANES].astype(bf16)
-        coef[mine, 1] = with_sums(sent[:, LANES:], sums()).astype(bf16)
+        coef[mine, 1] = with_sums(sent[:, LANES:], own_sums()).astype(bf16)
 
         for step in range(1, grp):
             send(
@@ -293,8 +299,7 @@
 
         after_send()
         before_near()
-        for l in range(leaves):
-            result[l] = nt(field[leaves + l], near_blocks[l, 0])
+        near_product(result, 0, 1, lambda l, k: field[leaves + l], False)
 
         if grp > 1:
             wait_bytes(coef.at[pl.ds(0, grp - 1)], coef_recv.at[phase, 1])
@@ -327,11 +332,11 @@
             wait_bytes(high, field_recv.at[phase, 1])
 
         first = me * leaves - leaves
-        for l in range(leaves):
-            total = result[l]
-            for k in range(1, near_count):
-                total = total + nt(field[jnp.clip(near_cols[l, k] - first, 0, 3 * leaves - 1)], near_blocks[l, k])
-            result[l] = total
+
+        def pick(l, k):
+            return field[jnp.clip(near_cols[l, k] - first, 0, 3 * leaves - 1)]
+
+        near_product(result, 1, near_count, pick, True)
 
         @pl.when(row > 0)
         def _():
@@ -346,23 +351,23 @@
 
         parts = []
         for l in range(leaves):
-            picked = jnp.concatenate(
+            taken = jnp.concatenate(
                 [
                     coef[slot(lax.div(leaf_far[l, k], leaves)), 0]
                     for k in range(leaf_slots)
                 ],
                 axis=1,
             )
-            parts.append(nt(picked, leaf_weights[l]))
+            parts.append(nt(taken, leaf_weights[l]))
         local = jnp.concatenate(parts, axis=1)
-        picked = jnp.concatenate(
+        taken = jnp.concatenate(
             [coef[slot(box_far[0, k]), 1] for k in range(box_slots)], axis=1
         )
-        local = local + nt(picked, box_weights[...])
+        local = local + nt(taken, box_weights[...])
         if rows > 1:
             wait_bytes(group.at[pl.ds(0, rows - 1)], group_recv.at[phase])
-        picked = jnp.concatenate([group[coarse_far[0, k]] for k in range(coarse_slots)], axis=1)
-        local = local + nt(picked, group_weights[...])
+        taken = jnp.concatenate([group[coarse_far[0, k]] for k in range(coarse_slots)], axis=1)
+        local = local + nt(taken, group_weights[...])
         far = jnp.dot(local.astype(bf16), receive_basis[...], preferred_element_type=f32)
         for l in range(leaves):
             result[l] = result[l] + far[:, l * cells : (l + 1) * cells]
@@ -396,37 +401,16 @@
         spread = jnp.zeros((rhs, LANES), f32)
         for n, column in enumerate(columns):
             spread = jnp.where(lane_at == sub_at + n * rhs, column, spread)
-        sums_a[z] = jnp.sum(spread, axis=0, keepdims=True)
-        for turn in range(1, grp):
-            send(
-                sums_a.at[z],
-                sums_a.at[z],
-                sums_send.at[0],
-                sums_recv.at[0],
-                row,
-                wrap(z + turn, grp),
-            )
+        sums[me] = jnp.sum(spread, axis=0, keepdims=True)
+
+        def send_sums(to_row, to_z):
+            send(sums.at[me], sums.at[me], sums_send, sums_recv, to_row, to_z)
+
+        each_other(send_sums)
 
     def finish_sums(count):
-        if grp > 1:
-            wait_bytes(sums_a.at[pl.ds(0, grp - 1)], sums_recv.at[0])
-        sums_b[row] = jnp.sum(sums_a[...], axis=0)
-
-        def send_sums(step, carry):
-            send(
-                sums_b.at[row],
-                sums_b.at[row],
-                sums_send.at[1],
-                sums_recv.at[1],
-                wrap(row + step, rows),
-                z,
-            )
-            return carry
-
-        lax.fori_loop(1, rows, send_sums, 0)
-        if rows > 1:
-            wait_bytes(sums_b.at[pl.ds(0, rows - 1)], sums_recv.at[1])
-        line = jnp.sum(sums_b[...], axis=0) / total_count
+        wait_bytes(sums.at[pl.ds(0, devices - 1)], sums_recv)
+        line = jnp.sum(sums[...], axis=0) / total_count
         spread = jnp.broadcast_to(line, (rhs, LANES))
         return [
             jnp.sum(jnp.where(lane_at == sub_at + n * rhs, spread, 0.0), axis=1, keepdims=True)
@@ -434,13 +418,13 @@
         ]
 
     def products(pairs):
-        sums = []
+        columns = []
         for left, right in pairs:
             total = left[0] * right[0]
             for l in range(1, leaves):
                 total = total + left[l] * right[l]
-            sums.append(jnp.sum(total, axis=1, keepdims=True))
-        return sums
+            columns.append(jnp.sum(total, axis=1, keepdims=True))
+        return columns
 
     def first_sums():
         return products([(vector, vector), (vector, image), (image, image)])
@@ -527,10 +511,7 @@
         hessenberg_out[n : n + 1, :] = line[:, :rhs]
     stores[2].start()
     drain(1, field_b, coef_b, group_b)
-    if grp > 1:
-        wait_bytes(sums_a.at[pl.ds(0, grp - 1)], sums_send.at[0])
-    if rows > 1:
-        wait_bytes(sums_b.at[pl.ds(0, rows - 1)], sums_send.at[1])
+    wait_bytes(sums.at[pl.ds(0, devices - 1)], sums_send)
     for store in stores:
         store.wait()
 
@@ -606,8 +587,7 @@
             pltpu.VMEM((3 * grp, 2, rhs, LANES), bf16),
             pltpu.VMEM((rows, rhs, LANES), bf16),
             pltpu.VMEM((rows, rhs, LANES), bf16),
-            pltpu.VMEM((grp, 1, LANES), f32),
-            pltpu.VMEM((rows, 1, LANES), f32),
+            pltpu.VMEM((rows * grp, 1, LANES), f32),
             pltpu.VMEM((2 * LANES, leaves * cells), bf16),
             pltpu.VMEM((LANES, leaves * cells), bf16),
             pltpu.VMEM((leaves, rank, leaf_far.shape[1] * LANES), bf16),
@@ -615,6 +595,7 @@
             pltpu.VMEM((LANES, coarse_far.shape[1] * LANES), bf16),
             pltpu.VMEM(vector.shape, f32),
             pltpu.VMEM(vector.shape, f32),
+            pltpu.VMEM((*near_blocks.shape[:2], leaves * rhs, cells), bf16),
             pltpu.VMEM((slots * rank, slots * LANES), bf16),
             pltpu.VMEM(vector.shape, f32),
             pltpu.VMEM(vector.shape, f32),
@@ -627,8 +608,8 @@
             dma((2, 3)),
             dma((2,)),
             dma((2,)),
-            dma((2,)),
-            dma((2,)),
+            dma(()),
+            dma(()),
         ],
         compiler_params=pltpu.CompilerParams(
             collective_id=0, has_side_effects=True, vmem_limit_bytes=65100 * 1024

time: 33.7 us -> 32.4 us (0.961)
  Pallas kernels: 32.9 us -> 31.6 us
    pallas_call x1, Pallas kernels: 31.3 us -> 29.9 us  [shards(): pl.pallas_call(functools.partial(kernel, rows, grp), out_shape=shapes, in...]
where the time goes in v4:
time: 32.4 us; the launch traced here: 32.2 us
  Pallas kernels  31.6 us (98%)
  between operations  0.64 us (2%)
    pallas_call x1, Pallas kernels, shards(): pl.pallas_call(functools.partial(kernel, rows, grp), out_shape=shapes, in...  29.9 us
    pallas_call x1, Pallas kernels, shards(): pl.pallas_call(hand_on, out_shape=shapes, in_specs=[hbm] * 3, out_specs=(...  1.63 us

profile of v4, /device:TPU:0, one launch (start us, length us, event | category | flops | bytes accessed | tf_op | source)
XLA Modules:
  0.0 32.2 jit_solution(13782764644938694803)
XLA Ops:
  0.6 29.9 %shard_map.148 = (f32[4,16,384]{2,1,0:T(8,128)}, f32[4,16,384]{2,1,0:T(8,128)}, f32[5,16]{1,0:T(8,128)}) custom-call(s32[4,3]{1,0:T(4,128)} %refs_0_.1, s32[4,8]{1,0:T(4,128)} %refs_1_.1, s32[1,4]{1,0:T(1,128)} %refs_2_.1, s32[1,4]{1,0:T(1,128)} %refs_3_.1, f32[4,16,384]{2,1,0:T(8,128)} %refs_4_.1, bf16[4,3,384,384]{3,2,1,0:T(8,128)(2,1)} %refs_5_.1, ...), custom_call_target="tpu_custom_call" | custom-call | tf_op jit(solution)/shard_map/pallas_call | solution.py:576
  30.6 1.6 %shard_map.149 = (f32[4,16,384]{2,1,0:T(8,128)}, f32[4,16,384]{2,1,0:T(8,128)}, f32[5,16]{1,0:T(8,128)}) custom-call(f32[4,16,384]{2,1,0:T(8,128)} %get-tuple-element.9.refs_0_, f32[4,16,384]{2,1,0:T(8,128)} %get-tuple-element.10.refs_1_, f32[5,16]{1,0:T(8,128)} %get-tuple-element.11.refs_2_), custom_call_target="tpu_custom_call" | custom-call | tf_op jit(solution)/shard_map/pallas_call | solution.py:618

commit v5 on v4

--- a/solution.py
+++ b/solution.py
@@ -234,6 +234,22 @@
         low = field.at[pl.ds(0, leaves)]
         high = field.at[pl.ds(2 * leaves, leaves)]
 
+        wide = jnp.concatenate([field[leaves + l] for l in range(leaves)], axis=1)
+        sent = nt(wide, send_basis[...])
+        mine = grp + z
+        coef[mine, 0] = sent[:, :LANES].astype(bf16)
+        coef[mine, 1] = with_sums(sent[:, LANES:], own_sums()).astype(bf16)
+
+        for step in range(1, grp):
+            send(
+                coef.at[mine],
+                coef.at[mine],
+                coef_send.at[phase, 1],
+                coef_recv.at[phase, 1],
+                row,
+                wrap(z + step, grp),
+            )
+
         @pl.when(me < devices - 1)
         def _():
             last = z == grp - 1
@@ -257,52 +273,36 @@
                 jnp.where(z == 0, grp - 1, z - 1),
             )
 
-        wide = jnp.concatenate([field[leaves + l] for l in range(leaves)], axis=1)
-        sent = nt(wide, send_basis[...])
-        mine = grp + z
-        coef[mine, 0] = sent[:, :LANES].astype(bf16)
-        coef[mine, 1] = with_sums(sent[:, LANES:], own_sums()).astype(bf16)
-
-        for step in range(1, grp):
-            send(
-                coef.at[mine],
-                coef.at[mine],
-                coef_send.at[phase, 1],
-                coef_recv.at[phase, 1],
-                row,
-                wrap(z + step, grp),
-            )
-
-        @pl.when(row > 0)
-        def _():
-            for other in range(grp):
-                send(
-                    coef.at[mine],
-                    coef.at[2 * grp + z],
-                    coef_send.at[phase, 0],
-                    coef_recv.at[phase, 2],
-                    row - 1,
-                    other,
-                )
-
-        @pl.when(row < rows - 1)
-        def _():
-            for other in range(grp):
-                send(
-                    coef.at[mine],
-                    coef.at[z],
-                    coef_send.at[phase, 2],
-                    coef_recv.at[phase, 0],
-                    row + 1,
-                    other,
-                )
-
         after_send()
         before_near()
         near_product(result, 0, 1, lambda l, k: field[leaves + l], False)
 
         if grp > 1:
             wait_bytes(coef.at[pl.ds(0, grp - 1)], coef_recv.at[phase, 1])
+        whole_row = coef.at[pl.ds(grp, grp)]
+
+        @pl.when(row > 0)
+        def _():
+            send(
+                whole_row,
+                coef.at[pl.ds(2 * grp, grp)],
+                coef_send.at[phase, 0],
+                coef_recv.at[phase, 2],
+                row - 1,
+                z,
+            )
+
+        @pl.when(row < rows - 1)
+        def _():
+            send(
+                whole_row,
+                coef.at[pl.ds(0, grp)],
+                coef_send.at[phase, 2],
+                coef_recv.at[phase, 0],
+                row + 1,
+                z,
+            )
+
         together = coef[grp, 1].astype(f32)
         for other in range(1, grp):
             together = together + coef[grp + other, 1].astype(f32)

time: 32.4 us -> 29.8 us (0.920)
  Pallas kernels: 31.6 us -> 29.1 us
    pallas_call x1, Pallas kernels: 29.9 us -> 27.4 us  [shards(): pl.pallas_call(functools.partial(kernel, rows, grp), out_shape=shapes, in...]
where the time goes in v5:
time: 29.8 us; the launch traced here: 29.7 us
  Pallas kernels  29.1 us (98%)
  between operations  0.64 us (2%)
    pallas_call x1, Pallas kernels, shards(): pl.pallas_call(functools.partial(kernel, rows, grp), out_shape=shapes, in...  27.4 us
    pallas_call x1, Pallas kernels, shards(): pl.pallas_call(hand_on, out_shape=shapes, in_specs=[hbm] * 3, out_specs=(...  1.63 us

profile of v5, /device:TPU:0, one launch (start us, length us, event | category | flops | bytes accessed | tf_op | source)
XLA Modules:
  0.0 29.7 jit_solution(15972393827919986745)
XLA Ops:
  0.6 27.4 %shard_map.148 = (f32[4,16,384]{2,1,0:T(8,128)}, f32[4,16,384]{2,1,0:T(8,128)}, f32[5,16]{1,0:T(8,128)}) custom-call(s32[4,3]{1,0:T(4,128)} %refs_0_.1, s32[4,8]{1,0:T(4,128)} %refs_1_.1, s32[1,4]{1,0:T(1,128)} %refs_2_.1, s32[1,4]{1,0:T(1,128)} %refs_3_.1, f32[4,16,384]{2,1,0:T(8,128)} %refs_4_.1, bf16[4,3,384,384]{3,2,1,0:T(8,128)(2,1)} %refs_5_.1, ...), custom_call_target="tpu_custom_call" | custom-call | tf_op jit(solution)/shard_map/pallas_call | solution.py:576
  28.1 1.6 %shard_map.149 = (f32[4,16,384]{2,1,0:T(8,128)}, f32[4,16,384]{2,1,0:T(8,128)}, f32[5,16]{1,0:T(8,128)}) custom-call(f32[4,16,384]{2,1,0:T(8,128)} %get-tuple-element.9.refs_0_, f32[4,16,384]{2,1,0:T(8,128)} %get-tuple-element.10.refs_1_, f32[5,16]{1,0:T(8,128)} %get-tuple-element.11.refs_2_), custom_call_target="tpu_custom_call" | custom-call | tf_op jit(solution)/shard_map/pallas_call | solution.py:618

commit v6 on v5

--- a/solution.py
+++ b/solution.py
@@ -125,14 +125,9 @@
     width = leaves * rank
     transfer = leaf_transfer[...].reshape(width, rank)
     down = jnp.dot(transfer, box_transfer[0], precision=highest, preferred_element_type=f32)
-    up = jnp.concatenate([transfer, down], axis=1).T
+    up = jnp.concatenate([transfer, down, jnp.zeros((width, LANES - 2 * rank), f32)], axis=1)
     up_high = up.astype(bf16)
     up_low = (up - up_high.astype(f32)).astype(bf16)
-    plain = send_basis[:width]
-    send_basis[width : width + 2 * rank] = (
-        jnp.dot(up_high, plain, preferred_element_type=f32)
-        + jnp.dot(up_low, plain, preferred_element_type=f32)
-    ).astype(bf16)
 
     def prepare_receive():
         for n in (7, 8, 10, 12, 0, 1, 2, 3):
@@ -228,17 +223,20 @@
     def operator(phase, source, result, field, coef, group, own_sums, after_send, before_near):
         for l in range(leaves):
             field[leaves + l] = source[l].astype(bf16)
-        if phase == 0:
-            pl.semaphore_wait(barrier, devices - 1)
         own = field.at[pl.ds(leaves, leaves)]
         low = field.at[pl.ds(0, leaves)]
         high = field.at[pl.ds(2 * leaves, leaves)]
 
         wide = jnp.concatenate([field[leaves + l] for l in range(leaves)], axis=1)
-        sent = nt(wide, send_basis[...])
+        sent = nt(wide, send_basis[...]).astype(bf16)
         mine = grp + z
-        coef[mine, 0] = sent[:, :LANES].astype(bf16)
-        coef[mine, 1] = with_sums(sent[:, LANES:], own_sums()).astype(bf16)
+        coef[mine, 0] = sent
+        upward = jnp.dot(sent, up_high, preferred_element_type=f32) + jnp.dot(
+            sent, up_low, preferred_element_type=f32
+        )
+        coef[mine, 1] = with_sums(upward, own_sums()).astype(bf16)
+        if phase == 0:
+            pl.semaphore_wait(barrier, devices - 1)
 
         for step in range(1, grp):
             send(
@@ -588,7 +586,7 @@
             pltpu.VMEM((rows, rhs, LANES), bf16),
             pltpu.VMEM((rows, rhs, LANES), bf16),
             pltpu.VMEM((rows * grp, 1, LANES), f32),
-            pltpu.VMEM((2 * LANES, leaves * cells), bf16),
+            pltpu.VMEM((LANES, leaves * cells), bf16),
             pltpu.VMEM((LANES, leaves * cells), bf16),
             pltpu.VMEM((leaves, rank, leaf_far.shape[1] * LANES), bf16),
             pltpu.VMEM((LANES, box_far.shape[1] * LANES), bf16),

time: 29.8 us -> 29.3 us (0.983)
  Pallas kernels: 29.1 us -> 28.5 us
    pallas_call x1, Pallas kernels: 27.4 us -> 26.8 us  [shards(): pl.pallas_call(functools.partial(kernel, rows, grp), out_shape=shapes, in...]
where the time goes in v6:
time: 29.3 us; the launch traced here: 29.1 us
  Pallas kernels  28.5 us (97%)
  between operations  0.64 us (2%)
    pallas_call x1, Pallas kernels, shards(): pl.pallas_call(functools.partial(kernel, rows, grp), out_shape=shapes, in...  26.8 us
    pallas_call x1, Pallas kernels, shards(): pl.pallas_call(hand_on, out_shape=shapes, in_specs=[hbm] * 3, out_specs=(...  1.63 us

profile of v6, /device:TPU:0, one launch (start us, length us, event | category | flops | bytes accessed | tf_op | source)
XLA Modules:
  0.0 29.1 jit_solution(4986219786934614081)
XLA Ops:
  0.6 26.8 %shard_map.148 = (f32[4,16,384]{2,1,0:T(8,128)}, f32[4,16,384]{2,1,0:T(8,128)}, f32[5,16]{1,0:T(8,128)}) custom-call(s32[4,3]{1,0:T(4,128)} %refs_0_.1, s32[4,8]{1,0:T(4,128)} %refs_1_.1, s32[1,4]{1,0:T(1,128)} %refs_2_.1, s32[1,4]{1,0:T(1,128)} %refs_3_.1, f32[4,16,384]{2,1,0:T(8,128)} %refs_4_.1, bf16[4,3,384,384]{3,2,1,0:T(8,128)(2,1)} %refs_5_.1, ...), custom_call_target="tpu_custom_call" | custom-call | tf_op jit(solution)/shard_map/pallas_call | solution.py:574
  27.5 1.6 %shard_map.149 = (f32[4,16,384]{2,1,0:T(8,128)}, f32[4,16,384]{2,1,0:T(8,128)}, f32[5,16]{1,0:T(8,128)}) custom-call(f32[4,16,384]{2,1,0:T(8,128)} %get-tuple-element.9.refs_0_, f32[4,16,384]{2,1,0:T(8,128)} %get-tuple-element.10.refs_1_, f32[5,16]{1,0:T(8,128)} %get-tuple-element.11.refs_2_), custom_call_target="tpu_custom_call" | custom-call | tf_op jit(solution)/shard_map/pallas_call | solution.py:616

commit v7 on v6

--- a/solution.py
+++ b/solution.py
@@ -271,7 +271,6 @@
                 jnp.where(z == 0, grp - 1, z - 1),
             )
 
-        after_send()
         before_near()
         near_product(result, 0, 1, lambda l, k: field[leaves + l], False)
 
@@ -320,6 +319,7 @@
             return carry
 
         lax.fori_loop(1, rows, send_group, 0)
+        after_send()
 
         @pl.when(me > 0)
         def _():

time: 29.3 us -> 29.3 us (level)
  no operation moved by 1% of the time
where the time goes in v7:
time: 29.3 us; the launch traced here: 29.1 us
  Pallas kernels  28.5 us (97%)
  between operations  0.64 us (2%)
    pallas_call x1, Pallas kernels, shards(): pl.pallas_call(functools.partial(kernel, rows, grp), out_shape=shapes, in...  26.8 us
    pallas_call x1, Pallas kernels, shards(): pl.pallas_call(hand_on, out_shape=shapes, in_specs=[hbm] * 3, out_specs=(...  1.63 us

profile of v7, /device:TPU:0, one launch (start us, length us, event | category | flops | bytes accessed | tf_op | source)
XLA Modules:
  0.0 29.1 jit_solution(11427748137518413827)
XLA Ops:
  0.6 26.8 %shard_map.148 = (f32[4,16,384]{2,1,0:T(8,128)}, f32[4,16,384]{2,1,0:T(8,128)}, f32[5,16]{1,0:T(8,128)}) custom-call(s32[4,3]{1,0:T(4,128)} %refs_0_.1, s32[4,8]{1,0:T(4,128)} %refs_1_.1, s32[1,4]{1,0:T(1,128)} %refs_2_.1, s32[1,4]{1,0:T(1,128)} %refs_3_.1, f32[4,16,384]{2,1,0:T(8,128)} %refs_4_.1, bf16[4,3,384,384]{3,2,1,0:T(8,128)(2,1)} %refs_5_.1, ...), custom_call_target="tpu_custom_call" | custom-call | tf_op jit(solution)/shard_map/pallas_call | solution.py:574
  27.5 1.6 %shard_map.149 = (f32[4,16,384]{2,1,0:T(8,128)}, f32[4,16,384]{2,1,0:T(8,128)}, f32[5,16]{1,0:T(8,128)}) custom-call(f32[4,16,384]{2,1,0:T(8,128)} %get-tuple-element.9.refs_0_, f32[4,16,384]{2,1,0:T(8,128)} %get-tuple-element.10.refs_1_, f32[5,16]{1,0:T(8,128)} %get-tuple-element.11.refs_2_), custom_call_target="tpu_custom_call" | custom-call | tf_op jit(solution)/shard_map/pallas_call | solution.py:616
